TPU v7x, 128 devices: a whole 4x4x4 slice. The times are simulated.
128 devices in a mesh: row: 8 (over x_lo, z), col: 16 (over x_hi, y, core).
Axes of the slice: x: 4 (x_hi: 2, x_lo: 2; x = x_hi * 2 + x_lo), y: 4, z: 4, core: 2. Of those that a mesh axis runs over, the one named last changes fastest.
Arguments:
- inverse_block: float32 [12288, 12288], P('row', 'col'), may hold values from -0.14433757 to 0.14433757, as said below
- grid_position: int32 [12288], replicated, may hold values from 0 to 12287, each once
- panel_a: float32 [512, 12288], P('row', 'col'), may hold values from -1.5 to 1.5
- pivot_inverse_a: float32 [512, 512], replicated, may hold values from -6 to 6
- chosen_rows: int32 [8192], replicated, may hold values from 0 to 12287, as said below
- top_panel_b: float32 [512, 512], replicated, may hold values from -1.5 to 1.5
- panel_b: float32 [512, 8192], P('row', 'col'), may hold values from -1.5 to 1.5
- pivot_inverse_b: float32 [512, 512], replicated, may hold values from -6 to 6
Outputs:
- inverse_panel_a: float32 [12288, 512], P(('row', 'col'))
- diagonal_a: float32 [512, 512], replicated
- inverse_panel_b: float32 [12288, 512], P(('row', 'col'))
- inverse_top_b: float32 [512, 512], replicated
- diagonal_b: float32 [512, 512], replicated
Inputs may be any that keep to these rules, and one draw needn't show every extreme that they name: `grid_position`: each of 0 to 12287 appears once. `chosen_rows`: 8192 distinct values. `inverse_block`: symmetric: entry (i, j) equals entry (j, i) in grid storage order.
All inputs are finite; a program needn't handle non-finite values.
Results may differ from a plain program's by a relative error of at most 0.00008.
Values sent between devices are 32-bit elements; how exact they have to be, the bound alone decides.
A program may use at most 128 MiB of HBM per device.

v0:
```python
import jax
import jax.numpy as jnp
from jax import lax
from jax.sharding import PartitionSpec as P


def pick_columns(wide, index, limit):
    valid = (index < limit).astype(jnp.float32)
    taken = jnp.take(wide, jnp.minimum(index, limit - 1), axis=1)
    return taken * valid[None, :]


def select_columns(wide, source, start, length, limit):
    index = lax.dynamic_slice_in_dim(source, start, length, 0)
    return pick_columns(wide, index, limit)


def project(block, panel_t):
    return lax.dot_general(
        block,
        panel_t,
        (((1,), (1,)), ((), ())),
        precision=lax.Precision.HIGHEST,
        preferred_element_type=jnp.float32,
    )


def body(
    inverse_block,
    grid_position,
    panel_a,
    pivot_inverse_a,
    chosen_rows,
    top_panel_b,
    panel_b,
    pivot_inverse_b,
):
    exact = lax.Precision.HIGHEST
    rows_here = inverse_block.shape[0]
    cols_here = inverse_block.shape[1]
    order = grid_position.shape[0]
    count = chosen_rows.shape[0]
    row_count = lax.axis_size("row")
    own_rows = rows_here // lax.axis_size("col")
    col_start = lax.axis_index("col") * cols_here
    own_start = lax.axis_index("row") * rows_here + lax.axis_index("col") * own_rows
    group_starts = (
        jnp.arange(row_count, dtype=jnp.int32) * rows_here + lax.axis_index("col") * own_rows
    )
    group_index = (group_starts[:, None] + jnp.arange(own_rows, dtype=jnp.int32)[None, :]).reshape(
        -1
    )
    local_offset = lax.axis_index("row") * own_rows
    source_a = (
        jnp.zeros((order,), jnp.int32).at[grid_position].set(jnp.arange(order, dtype=jnp.int32))
    )
    source_b = (
        jnp.full((order,), count, jnp.int32)
        .at[grid_position[chosen_rows]]
        .set(jnp.arange(count, dtype=jnp.int32))
    )
    group_a = source_a[group_index]
    group_b = source_b[group_index]
    valid_own = (lax.dynamic_slice_in_dim(source_b, own_start, own_rows, 0) < count).astype(
        jnp.float32
    )
    wide_a = lax.all_gather(panel_a, "col", axis=1, tiled=True)
    cols_a, group_own_a = (
        lax.all_gather(
            select_columns(wide_a, source_a, col_start, cols_here, order), "row", axis=0, tiled=True
        ),
        lax.all_gather(pick_columns(wide_a, group_a, order), "row", axis=0, tiled=True),
    )
    product_a = lax.psum_scatter(
        project(inverse_block, cols_a), "col", scatter_dimension=0, tiled=True
    )
    wide_b = lax.all_gather(panel_b, "col", axis=1, tiled=True)
    cols_b, group_own_b = (
        lax.all_gather(
            select_columns(wide_b, source_b, col_start, cols_here, count), "row", axis=0, tiled=True
        ),
        lax.all_gather(pick_columns(wide_b, group_b, count), "row", axis=0, tiled=True),
    )
    product_b = lax.psum_scatter(
        project(inverse_block, cols_b), "col", scatter_dimension=0, tiled=True
    )
    own_a = lax.dynamic_slice_in_dim(group_own_a, local_offset, own_rows, 1)
    own_b = lax.dynamic_slice_in_dim(group_own_b, local_offset, own_rows, 1)
    inverse_panel_a = -product_a
    diag_part = jnp.dot(own_a, inverse_panel_a, precision=exact, preferred_element_type=jnp.float32)
    cross_part = lax.dot_general(
        inverse_panel_a,
        own_b,
        (((0,), (1,)), ((), ())),
        precision=exact,
        preferred_element_type=jnp.float32,
    )
    diag_total, cross = lax.psum((diag_part, cross_part), ("row", "col"))
    diagonal_a = pivot_inverse_a - diag_total
    inverse_top_b = -(
        jnp.dot(diagonal_a, top_panel_b, precision=exact, preferred_element_type=jnp.float32)
        + cross
    )
    bottom = product_b + jnp.dot(
        inverse_panel_a, top_panel_b, precision=exact, preferred_element_type=jnp.float32
    )
    inverse_panel_b = -bottom * valid_own[:, None]
    last_part = jnp.dot(own_b, inverse_panel_b, precision=exact, preferred_element_type=jnp.float32)
    last_total = lax.psum(last_part, ("row", "col"))
    diagonal_b = (
        pivot_inverse_b
        - jnp.dot(top_panel_b.T, inverse_top_b, precision=exact, preferred_element_type=jnp.float32)
        - last_total
    )
    return (inverse_panel_a, diagonal_a, inverse_panel_b, inverse_top_b, diagonal_b)


def solution(mesh):
    in_specs = (P("row", "col"), P(), P("row", "col"), P(), P(), P(), P("row", "col"), P())
    out_specs = (P(("row", "col"), None), P(), P(("row", "col"), None), P(), P())
    return jax.shard_map(body, mesh=mesh, in_specs=in_specs, out_specs=out_specs, check_vma=False)
```

profile of v0, /device:TPU:1, one launch (start us, length us, event | category | flops | bytes accessed | tf_op | source)
XLA Modules:
  0.0 630.5 jit_solution(11764547674448368654)
XLA Ops:
  11.9 45.4 %scatter_custom_fusion = s32[12288]{0:T(1024)S(1)} fusion(s32[12288]{0:T(1024)S(1)} %compare_select_fusion.1, s32[12288]{0:T(1024)S(1)} %iota.15, s32[]{:T(128)} %constant.4.clone.1), kind=kCustom, calls=%fused_computation.35 | custom fusion | bytes 49156 | tf_op jit(solution)/shard_map/scatter | solution.py:55
  57.4 21.3 %all-gather.7.cloned.1.call-done = f32[64,12288]{0,1:T(8,128)} async-done(((f32[64,768]{0,1:T(8,128)}), f32[64,12288]{0,1:T(8,128)}) %all-gather.7.cloned.1.call-update) | async-done | bytes 3145744 | tf_op jit(solution)/shard_map/all_gather | solution.py:67
  78.7 4.3 gather_fusion.3
  84.1 45.5 %gather_fusion.1 = s32[8192]{0:T(1024)S(1)} fusion(s32[12288]{0:T(1024)S(1)} %copy-done.1, s32[8192]{0:T(1024)S(1)} %fusion.11), kind=kCustom, calls=%fused_computation.5 | custom fusion | bytes 98304 | tf_op jit(solution)/shard_map/gather | solution.py:59
  129.7 30.5 %scatter_custom_fusion.1 = s32[12288]{0:T(1024)S(1)} fusion(s32[8192]{0:T(1024)S(1)} %bitcast.35, s32[8192]{0:T(1024)S(1)} %iota.17, s32[]{:T(128)} %constant.36.clone.1), kind=kCustom, calls=%fused_computation.33 | custom fusion | bytes 49156 | tf_op jit(solution)/shard_map/scatter | solution.py:60
  160.3 3.8 gather_fusion.5
  165.0 4.1 all-gather.9.cloned.1.call-done
  169.1 11.3 %convolution_bitcast_fusion.1 = f32[1536,512]{0,1:T(8,128)} fusion(f32[512,768]{1,0:T(8,128)} %all-gather.9.cloned.1.call-done, f32[1536,768]{1,0:T(8,128)} %param.12), kind=kOutput, calls=%fused_computation.10 | convolution fusion | flops 7247757312 | bytes 9437184 | tf_op jit(solution)/shard_map/dot_general | solution.py:19
  180.3 3.7 copy.52
  184.3 4.5 gather_fusion
  188.8 4.4 gather_fusion.4
  194.1 4.5 gather_fusion.2
  198.6 3.8 gather_fusion.6
  203.5 7.6 %all-gather.15.cloned.1.call-done = f32[512,768]{1,0:T(8,128)} async-done(((f32[64,768]{1,0:T(8,128)}), f32[512,768]{1,0:T(8,128)}) %all-gather.15.cloned.1.call-update) | async-done | bytes 1572880 | tf_op jit(solution)/shard_map/all_gather | solution.py:79
  211.0 11.3 %convolution_bitcast_fusion = f32[1536,512]{0,1:T(8,128)} fusion(f32[512,768]{1,0:T(8,128)} %all-gather.15.cloned.1.call-done, f32[1536,768]{1,0:T(8,128)} %param.12), kind=kOutput, calls=%fused_computation.9 | convolution fusion | flops 7247757312 | bytes 9437184 | tf_op jit(solution)/shard_map/dot_general | solution.py:19
  222.4 3.5 copy.54
  226.0 68.4 %reduce-scatter.7.cloned.1.call-done = f32[96,512]{1,0:T(8,128)} async-done(((f32[1536,512]{1,0:T(8,128)}), f32[96,512]{1,0:T(8,128)}) %reduce-scatter.7.cloned.1.call-update) | async-done | bytes 196624
  295.5 35.6 %all-gather.11.cloned.1.call-done = f32[512,768]{1,0:T(8,128)} async-done(((f32[64,768]{1,0:T(8,128)}), f32[512,768]{1,0:T(8,128)}) %all-gather.11.cloned.1.call-update) | async-done | bytes 1572880 | tf_op jit(solution)/shard_map/all_gather | solution.py:72
  331.1 3.0 fusion.5
  334.1 39.1 %all-gather.17.cloned.1.call-done = f32[512,768]{1,0:T(8,128)} async-done(((f32[64,768]{1,0:T(8,128)}), f32[512,768]{1,0:T(8,128)}) %all-gather.17.cloned.1.call-update) | async-done | bytes 1572880 | tf_op jit(solution)/shard_map/all_gather | solution.py:82
  373.2 3.1 fusion.9
  376.3 80.5 %reduce-scatter.9.cloned.1.call-done = f32[96,512]{1,0:T(8,128)} async-done(((f32[1536,512]{1,0:T(8,128)}), f32[96,512]{1,0:T(8,128)}) %reduce-scatter.9.cloned.1.call-update) | async-done | bytes 196624 | tf_op jit(solution)/shard_map/reduce_scatter | solution.py:84
  459.2 3.1 fusion.7
  466.5 149.7 %all-reduce.3.cloned.1.call-done = (f32[512,512]{1,0:T(8,128)}, f32[512,512]{1,0:T(8,128)}, f32[512,512]{0,1:T(8,128)}) async-done(((f32[512,512]{1,0:T(8,128)}, f32[512,512]{1,0:T(8,128)}, f32[512,512]{0,1:T(8,128)}), (f32[512,512]{1,0:T(8,128)}, f32[512,512]{1,0:T(8,128)}, f32[512,512]{0,1:T(8,128)})) %all-reduce.3.cloned.1.call-update) | async-done | bytes 3145744 | tf_op jit(solution)/shard_map/psum | solution.py:98
  (77 shorter events, 24.3 us)
Async XLA Ops:
  7.2 449.7 %copy-start = (f32[512,512]{1,0:T(8,128)S(1)}, f32[512,512]{1,0:T(8,128)}, u32[]{:S(2)}) copy-start(f32[512,512]{1,0:T(8,128)} %param.17) | copy-start | bytes 3145732
  7.2 76.9 %copy-start.1 = (s32[12288]{0:T(1024)S(1)}, s32[12288]{0:T(1024)}, u32[]{:S(2)}) copy-start(s32[12288]{0:T(1024)} %param.13) | copy-start | bytes 147460
  7.2 76.8 %copy-start.8 = (s32[8192]{0:T(1024)S(1)}, s32[8192]{0:T(1024)}, u32[]{:S(2)}) copy-start(s32[8192]{0:T(1024)} %param.16) | copy-start | bytes 98308
  7.2 71.5 %all-gather.7.cloned.1.call-start = ((), (), s32[]{:S(2)}) async-start(), calls=%async_computation.2 | async-start | bytes 6684672 | tf_op jit(solution)/shard_map/all_gather | solution.py:67
  9.2 151.1 %all-gather.13.cloned.1.call-start = ((), (), s32[]{:S(2)}) async-start(), calls=%async_computation.5 | async-start | bytes 4456448 | tf_op jit(solution)/shard_map/all_gather | solution.py:77
  11.0 158.0 %all-gather.9.cloned.1.call-start = ((), (), s32[]{:S(2)}) async-start(), calls=%async_computation.3 | async-start | bytes 1769472 | tf_op jit(solution)/shard_map/all_gather | solution.py:69
  84.0 127.1 %all-gather.15.cloned.1.call-start = ((), (), s32[]{:S(2)}) async-start(), calls=%async_computation.6 | async-start | bytes 1769472 | tf_op jit(solution)/shard_map/all_gather | solution.py:79
  164.9 129.5 %reduce-scatter.7.cloned.1.call-start = ((), (), s32[]{:S(2)}) async-start(), calls=%async_computation.8 | async-start | bytes 3342336
  184.0 147.1 %all-gather.11.cloned.1.call-start = ((), (), s32[]{:S(2)}) async-start(), calls=%async_computation.4 | async-start | bytes 1769472 | tf_op jit(solution)/shard_map/all_gather | solution.py:72
  194.0 179.2 %all-gather.17.cloned.1.call-start = ((), (), s32[]{:S(2)}) async-start(), calls=%async_computation.7 | async-start | bytes 1769472 | tf_op jit(solution)/shard_map/all_gather | solution.py:82
  203.3 253.6 %reduce-scatter.9.cloned.1.call-start = ((), (), s32[]{:S(2)}) async-start(), calls=%async_computation.9 | async-start | bytes 3342336 | tf_op jit(solution)/shard_map/reduce_scatter | solution.py:84
  225.9 390.3 %all-reduce.3.cloned.1.call-start = ((), (), s32[]{:S(2)}) async-start(), calls=%async_computation.10 | async-start | bytes 6291456 | tf_op jit(solution)/shard_map/psum | solution.py:98
  458.5 0.7 copy-start.7
  462.3 153.9 %copy-start.4 = (f32[512,512]{1,0:T(8,128)S(1)}, f32[512,512]{1,0:T(8,128)}, u32[]{:S(2)}) copy-start(f32[512,512]{1,0:T(8,128)} %param.15) | copy-start | bytes 3145732
  616.2 1.6 copy-start.6
  616.2 4.5 copy-start.5
  617.7 1.9 copy-start.2
  619.6 1.0 copy-start.3
Sparse Core Ops, SparseCore 0:
  11.1 67.6 all-gather.6
  81.8 53.0 all-gather.12
  137.1 31.9 all-gather.8
  171.1 39.8 all-gather.14
  214.9 79.4 reduce-scatter.6
  296.5 34.5 all-gather.10
  333.3 39.8 all-gather.16
  377.3 79.5 reduce-scatter.8
  462.5 153.5 all-reduce.2
where the time goes:
time: 631 us; the launch traced here: 630 us
  waiting for transfers between devices  406 us (64%)
  local copies, waits for them, and re-layouts  166 us (26%)
  matrix products  37.4 us (6%)
  between operations  14.2 us (2%)
  other arithmetic  6.35 us (1%)
    psum x1, waiting for transfers between devices, body(): diag_total, cross = lax.psum((diag_part, cross_part), ('row', 'col'))  150 us
    reduce_scatter x1, waiting for transfers between devices, body(): lax.psum_scatter(project(inverse_block, cols_b), 'col', scatter_dimension...  80.5 us
    unnamed x10, waiting for transfers between devices  68.6 us
    gather x1, local copies, waits for them, and re-layouts, body(): grid_position[chosen_rows]  45.5 us
    scatter x1, local copies, waits for them, and re-layouts, body(): jnp.zeros((order,), jnp.int32).at[grid_position]  45.4 us
    all_gather x1, waiting for transfers between devices, body(): lax.all_gather(pick_columns(wide_b, group_b, count), 'row', axis=0, tiled...  39.1 us
    all_gather x1, waiting for transfers between devices, body(): lax.all_gather(pick_columns(wide_a, group_a, order), 'row', axis=0, tiled...  35.6 us
    scatter x1, local copies, waits for them, and re-layouts, body(): source_b = jnp.full((order,), count, jnp.int32).at[grid_position[chosen_r...  30.5 us
  transfers between devices with their start and end apart: 9, of which 8 were waited for; matrix products, arithmetic and copies ran while one was open for 31% of the time, Pallas kernels for 0%

commit v1 on v0

--- a/solution.py
+++ b/solution.py
@@ -95,7 +95,9 @@
         precision=exact,
         preferred_element_type=jnp.float32,
     )
-    diag_total, cross = lax.psum((diag_part, cross_part), ("row", "col"))
+    diag_total, cross = lax.psum(
+        lax.psum((diag_part, cross_part), axis_name="col"), axis_name="row"
+    )
     diagonal_a = pivot_inverse_a - diag_total
     inverse_top_b = -(
         jnp.dot(diagonal_a, top_panel_b, precision=exact, preferred_element_type=jnp.float32)

time: 631 us -> 858 us (1.36)
  waiting for transfers between devices: 406 us -> 632 us
    psum x1 -> x3, waiting for transfers between devices: 150 us -> 361 us  [the longest x1 151 us: body(): last_total = lax.psum(last_part, ('row', 'col'))]
    unnamed x10 -> x12, waiting for transfers between devices: 68.6 us -> 24.3 us
    all_gather x1, waiting for transfers between devices: 7.55 us -> 38.9 us  [body(): lax.all_gather(select_columns(wide_b, source_b, col_start, cols_here, cou...]
    all_gather x1, waiting for transfers between devices: 4.08 us -> 31.1 us  [body(): lax.all_gather(select_columns(wide_a, source_a, col_start, cols_here, ord...]
    unnamed x26 -> x24, local copies, waits for them, and re-layouts: 18.2 us -> 16.6 us
  transfers between devices with their start and end apart: 9 -> 11, of which waited for: 8 -> 10; matrix products, arithmetic and copies ran while one was open for 31% -> 23% of each run, Pallas kernels for 0% -> 0%
where the time goes in v1:
time: 858 us
  waiting for transfers between devices  632 us (74%)
  local copies, waits for them, and re-layouts  164 us (19%)
  matrix products  40 us (5%)
  between operations  14.2 us (2%)
    psum x1, waiting for transfers between devices, body(): last_total = lax.psum(last_part, ('row', 'col'))  151 us
    psum x1, waiting for transfers between devices, body(): lax.psum((diag_part, cross_part), axis_name='col')  137 us
    reduce_scatter x1, waiting for transfers between devices, body(): lax.psum_scatter(project(inverse_block, cols_b), 'col', scatter_dimension...  79.1 us
    psum x1, waiting for transfers between devices, body(): lax.psum(lax.psum((diag_part, cross_part), axis_name='col'), axis_name='r...  72.3 us
    gather x1, local copies, waits for them, and re-layouts, body(): grid_position[chosen_rows]  45.5 us
    scatter x1, local copies, waits for them, and re-layouts, body(): jnp.zeros((order,), jnp.int32).at[grid_position]  45.4 us
    all_gather x1, waiting for transfers between devices, body(): lax.all_gather(select_columns(wide_b, source_b, col_start, cols_here, cou...  38.9 us
    all_gather x1, waiting for transfers between devices, body(): lax.all_gather(pick_columns(wide_b, group_b, count), 'row', axis=0, tiled...  38.9 us
  transfers between devices with their start and end apart: 11, of which 10 were waited for; matrix products, arithmetic and copies ran while one was open for 23% of the time, Pallas kernels for 0%

profile of v1, /device:TPU:1, one launch (start us, length us, event | category | flops | bytes accessed | tf_op | source)
XLA Modules:
  0.0 857.6 jit_solution(6523447706915437993)
XLA Ops:
  10.1 45.4 %scatter_custom_fusion = s32[12288]{0:T(1024)S(1)} fusion(s32[12288]{0:T(1024)S(1)} %compare_select_fusion.1, s32[12288]{0:T(1024)S(1)} %iota.15, s32[]{:T(128)} %constant.4.clone.1), kind=kCustom, calls=%fused_computation.35 | custom fusion | bytes 49156 | tf_op jit(solution)/shard_map/scatter | solution.py:55
  55.6 23.1 %all-gather.7.cloned.1.call-done = f32[64,12288]{0,1:T(8,128)} async-done(((f32[64,768]{0,1:T(8,128)}), f32[64,12288]{0,1:T(8,128)}) %all-gather.7.cloned.1.call-update) | async-done | bytes 3145744 | tf_op jit(solution)/shard_map/all_gather | solution.py:67
  78.7 4.3 gather_fusion.3
  84.9 31.1 %all-gather.9.cloned.1.call-done = f32[512,768]{1,0:T(8,128)} async-done(((f32[64,768]{1,0:T(8,128)}), f32[512,768]{1,0:T(8,128)}) %all-gather.9.cloned.1.call-update) | async-done | bytes 1572880 | tf_op jit(solution)/shard_map/all_gather | solution.py:69
  116.0 11.3 %convolution_bitcast_fusion.1 = f32[1536,512]{0,1:T(8,128)} fusion(f32[512,768]{1,0:T(8,128)} %all-gather.9.cloned.1.call-done, f32[1536,768]{1,0:T(8,128)} %param.12), kind=kOutput, calls=%fused_computation.10 | convolution fusion | flops 7247757312 | bytes 9437184 | tf_op jit(solution)/shard_map/dot_general | solution.py:19
  127.4 3.7 copy.52
  131.4 4.5 gather_fusion
  135.9 4.4 gather_fusion.4
  141.2 45.5 %gather_fusion.1 = s32[8192]{0:T(1024)S(1)} fusion(s32[12288]{0:T(1024)S(1)} %copy-done.1, s32[8192]{0:T(1024)S(1)} %fusion.11), kind=kCustom, calls=%fused_computation.5 | custom fusion | bytes 98304 | tf_op jit(solution)/shard_map/gather | solution.py:59
  186.8 30.5 %scatter_custom_fusion.1 = s32[12288]{0:T(1024)S(1)} fusion(s32[8192]{0:T(1024)S(1)} %bitcast.35, s32[8192]{0:T(1024)S(1)} %iota.17, s32[]{:T(128)} %constant.36.clone.1), kind=kCustom, calls=%fused_computation.33 | custom fusion | bytes 49156 | tf_op jit(solution)/shard_map/scatter | solution.py:60
  217.3 4.5 gather_fusion.2
  221.8 3.8 gather_fusion.6
  226.6 3.8 gather_fusion.5
  231.5 24.1 %reduce-scatter.7.cloned.1.call-done = f32[96,512]{1,0:T(8,128)} async-done(((f32[1536,512]{1,0:T(8,128)}), f32[96,512]{1,0:T(8,128)}) %reduce-scatter.7.cloned.1.call-update) | async-done | bytes 196624
  256.7 35.6 %all-gather.11.cloned.1.call-done = f32[512,768]{1,0:T(8,128)} async-done(((f32[64,768]{1,0:T(8,128)}), f32[512,768]{1,0:T(8,128)}) %all-gather.11.cloned.1.call-update) | async-done | bytes 1572880 | tf_op jit(solution)/shard_map/all_gather | solution.py:72
  295.3 38.9 %all-gather.17.cloned.1.call-done = f32[512,768]{1,0:T(8,128)} async-done(((f32[64,768]{1,0:T(8,128)}), f32[512,768]{1,0:T(8,128)}) %all-gather.17.cloned.1.call-update) | async-done | bytes 1572880 | tf_op jit(solution)/shard_map/all_gather | solution.py:82
  337.4 38.9 %all-gather.15.cloned.1.call-done = f32[512,768]{1,0:T(8,128)} async-done(((f32[64,768]{1,0:T(8,128)}), f32[512,768]{1,0:T(8,128)}) %all-gather.15.cloned.1.call-update) | async-done | bytes 1572880 | tf_op jit(solution)/shard_map/all_gather | solution.py:79
  376.3 11.4 %convolution_bitcast_fusion = f32[1536,512]{0,1:T(8,128)} fusion(f32[512,768]{1,0:T(8,128)} %all-gather.15.cloned.1.call-done, f32[1536,768]{1,0:T(8,128)} %param.12), kind=kOutput, calls=%fused_computation.9 | convolution fusion | flops 7247757312 | bytes 9437184 | tf_op jit(solution)/shard_map/dot_general | solution.py:19
  387.7 3.5 copy.54
  391.3 137.5 %all-reduce.8.cloned.1.call-done = (f32[512,512]{1,0:T(8,128)}, f32[512,512]{1,0:T(8,128)}) async-done(((f32[512,512]{1,0:T(8,128)}, f32[512,512]{1,0:T(8,128)}), (f32[512,512]{1,0:T(8,128)}, f32[512,512]{1,0:T(8,128)})) %all-reduce.8.cloned.1.call-update) | async-done | bytes 2097168 | tf_op jit(solution)/shard_map/psum | solution.py:99
  529.2 79.1 %reduce-scatter.9.cloned.1.call-done = f32[96,512]{1,0:T(8,128)} async-done(((f32[1536,512]{1,0:T(8,128)}), f32[96,512]{1,0:T(8,128)}) %reduce-scatter.9.cloned.1.call-update) | async-done | bytes 196624 | tf_op jit(solution)/shard_map/reduce_scatter | solution.py:84
  617.3 72.3 %all-reduce.10.cloned.1.call-done = (f32[512,512]{1,0:T(8,128)}, f32[512,512]{1,0:T(8,128)}) async-done(((f32[512,512]{1,0:T(8,128)}, f32[512,512]{1,0:T(8,128)}), (f32[512,512]{1,0:T(8,128)}, f32[512,512]{1,0:T(8,128)})) %all-reduce.10.cloned.1.call-update) | async-done | bytes 2097168 | tf_op jit(solution)/shard_map/psum | solution.py:98
  694.9 151.5 %all-reduce.6.cloned.1.call-done = f32[512,512]{0,1:T(8,128)} async-done(((f32[512,512]{0,1:T(8,128)}), f32[512,512]{0,1:T(8,128)}) %all-reduce.6.cloned.1.call-update) | async-done | bytes 1048592 | tf_op jit(solution)/shard_map/psum | solution.py:111
  846.3 3.4 fusion.1
  (81 shorter events, 31.3 us)
Async XLA Ops:
  7.2 601.1 %copy-start = (f32[512,512]{1,0:T(8,128)S(1)}, f32[512,512]{1,0:T(8,128)}, u32[]{:S(2)}) copy-start(f32[512,512]{1,0:T(8,128)} %param.17) | copy-start | bytes 3145732
  7.2 76.8 %copy-start.6 = (f32[64,512]{1,0:T(8,128)S(1)}, f32[64,512]{1,0:T(8,128)}, u32[]{:S(2)}) copy-start(f32[64,512]{1,0:T(8,128)} %param.18) | copy-start | bytes 393220
  7.2 71.5 %all-gather.7.cloned.1.call-start = ((), (), s32[]{:S(2)}) async-start(), calls=%async_computation.2 | async-start | bytes 6684672 | tf_op jit(solution)/shard_map/all_gather | solution.py:67
  9.2 106.9 %all-gather.9.cloned.1.call-start = ((), (), s32[]{:S(2)}) async-start(), calls=%async_computation.3 | async-start | bytes 1769472 | tf_op jit(solution)/shard_map/all_gather | solution.py:69
  84.0 137.8 %all-gather.13.cloned.1.call-start = ((), (), s32[]{:S(2)}) async-start(), calls=%async_computation.5 | async-start | bytes 4456448 | tf_op jit(solution)/shard_map/all_gather | solution.py:77
  84.9 170.7 %reduce-scatter.7.cloned.1.call-start = ((), (), s32[]{:S(2)}) async-start(), calls=%async_computation.9 | async-start | bytes 3342336
  131.1 161.2 %all-gather.11.cloned.1.call-start = ((), (), s32[]{:S(2)}) async-start(), calls=%async_computation.4 | async-start | bytes 1769472 | tf_op jit(solution)/shard_map/all_gather | solution.py:72
  131.3 9.8 %copy-start.7 = (s32[8192]{0:T(1024)S(1)}, s32[8192]{0:T(1024)}, u32[]{:S(2)}) copy-start(s32[8192]{0:T(1024)} %param.16) | copy-start | bytes 98308
  131.3 9.8 %copy-start.1 = (s32[12288]{0:T(1024)S(1)}, s32[12288]{0:T(1024)}, u32[]{:S(2)}) copy-start(s32[12288]{0:T(1024)} %param.13) | copy-start | bytes 147460
  141.1 193.1 %all-gather.17.cloned.1.call-start = ((), (), s32[]{:S(2)}) async-start(), calls=%async_computation.7 | async-start | bytes 1769472 | tf_op jit(solution)/shard_map/all_gather | solution.py:82
  226.5 149.9 %all-gather.15.cloned.1.call-start = ((), (), s32[]{:S(2)}) async-start(), calls=%async_computation.6 | async-start | bytes 1769472 | tf_op jit(solution)/shard_map/all_gather | solution.py:79
  231.3 297.5 %all-reduce.8.cloned.1.call-start = ((), (), s32[]{:S(2)}) async-start(), calls=%async_computation.11 | async-start | bytes 4194304 | tf_op jit(solution)/shard_map/psum | solution.py:99
  337.3 270.9 %reduce-scatter.9.cloned.1.call-start = ((), (), s32[]{:S(2)}) async-start(), calls=%async_computation.10 | async-start | bytes 3342336 | tf_op jit(solution)/shard_map/reduce_scatter | solution.py:84
  391.3 298.2 %all-reduce.10.cloned.1.call-start = ((), (), s32[]{:S(2)}) async-start(), calls=%async_computation.12 | async-start | bytes 4194304 | tf_op jit(solution)/shard_map/psum | solution.py:98
  528.8 317.5 %all-reduce.6.cloned.1.call-start = ((), (), s32[]{:S(2)}) async-start(), calls=%async_computation.8 | async-start | bytes 2097152 | tf_op jit(solution)/shard_map/psum | solution.py:111
  609.9 3.2 copy-start.5
  610.0 79.6 %copy-start.3 = (f32[512,512]{1,0:T(8,128)S(1)}, f32[512,512]{1,0:T(8,128)}, u32[]{:S(2)}) copy-start(f32[512,512]{1,0:T(8,128)} %param.15) | copy-start | bytes 3145732
  689.5 2.5 copy-start.4
  691.1 1.0 copy-start.2
Sparse Core Ops, SparseCore 0:
  11.1 67.6 all-gather.6
  84.1 31.9 all-gather.8
  119.1 60.9 all-gather.12
  184.0 71.5 reduce-scatter.6
  257.7 34.5 all-gather.10
  294.3 39.8 all-gather.16
  336.4 39.8 all-gather.14
  379.4 149.3 all-reduce.7
  532.9 75.3 reduce-scatter.8
  610.7 78.8 all-reduce.9
  694.9 151.3 all-reduce.5
